TPU v7x, 256 devices: a whole 4x4x8 slice. The times are simulated.
256 devices in a mesh: dp: 32 (over y, z_lo, core), tensor: 8 (over z_hi, x).
Axes of the slice: x: 4, y: 4, z: 8 (z_hi: 2, z_lo: 4; z = z_hi * 4 + z_lo), core: 2. Of those that a mesh axis runs over, the one named last changes fastest.
Arguments:
- stream_in: bfloat16 [4096, 4096], P(('dp', 'tensor')), may hold values from -6 to 6
- pending: bfloat16 [8, 4096, 4096], P('tensor', 'dp'), may hold values from -6 to 6
- gain: float32 [4096], replicated, may hold values from 0.5 to 1.5
- q_weight: bfloat16 [4096, 4096], P('dp', 'tensor'), may hold values from -1 to 1
- k_weight: bfloat16 [4096, 512], P('dp'), may hold values from -4 to 4
- v_weight: bfloat16 [4096, 512], P('dp'), may hold values from -0.09375 to 0.09375
- out_weight: bfloat16 [4096, 4096], P('dp', 'tensor'), may hold values from -0.09375 to 0.09375
- grad_out: bfloat16 [4096, 4096], P(('dp', 'tensor')), may hold values from -6 to 6
- doc_ids: int32 [4096], replicated, may hold values from 0 to 5, never falling along the last dimension, each value on 1 to 3072 neighbouring positions
Outputs:
- hidden_out: bfloat16 [4096, 4096], P(('dp', 'tensor'))
- grad_stream: bfloat16 [4096, 4096], P(('dp', 'tensor'))
- grad_gain: float32 [4096], replicated
- grad_q: float32 [4096, 4096], P('dp', 'tensor')
- grad_k: float32 [4096, 512], P('dp')
- grad_v: float32 [4096, 512], P('dp')
- grad_o: float32 [4096, 4096], P('dp', 'tensor')
Inputs may be any that keep to these rules, and one draw needn't show every extreme that they name: `doc_ids`: never falls along the positions; the longest document has exactly 3072 positions.
All inputs are finite; a program needn't handle non-finite values.
Results may differ from a plain program's by a relative error of at most 0.035.
The roundings to bfloat16 on the way count: a program that leaves them out, or rounds other values in their place, can miss the bound.
Values may be sent and summed in bfloat16 or wider, within the bound.
No kernel may reach another device: no remote copies, remote signals or barrier semaphores. Data moves between devices by JAX's collectives and lax.ppermute only.
A program may use at most 128 MiB of HBM per device.

v0:
```python
import jax
import jax.numpy as jnp
from jax import lax
from jax.sharding import PartitionSpec as P

HEADS = 32
KV_HEADS = 4
HEAD_DIM = 128


eps = 1e-05
rope_base = 500000.0


def rotate(field, positions, sign):
    half = field.shape[-1] // 2
    frequency = rope_base ** (-2.0 * jnp.arange(half).astype(field.dtype) / field.shape[-1])
    angles = positions.astype(field.dtype)[:, None] * frequency[None, :]
    cosine = jnp.cos(angles)[:, None, :]
    sine = sign * jnp.sin(angles)[:, None, :]
    first = field[..., :half]
    second = field[..., half:]
    return jnp.concatenate(
        [first * cosine - second * sine, second * cosine + first * sine], axis=-1
    )


def window_keys(field, offset, count, total):
    padded = jnp.pad(field, ((0, 0), (0, 0), (0, 0), (count, count)))
    begin = jnp.clip(offset + count, 0, total + count)
    return lax.dynamic_slice_in_dim(padded, begin, count, 3)


def on_device(
    stream_in, pending, gain, q_weight, k_weight, v_weight, out_weight, grad_out, doc_ids
):
    f_wide = jnp.float32
    f_low = jnp.bfloat16
    tens_index = lax.axis_index("tensor")
    data_index = lax.axis_index("dp")
    tens_count = lax.axis_size("tensor")
    data_count = lax.axis_size("dp")
    tok_block = pending.shape[1]
    seq_len = tok_block * data_count
    q_width = q_weight.shape[1]
    q_local = q_width // HEAD_DIM
    kv_local = max(KV_HEADS // tens_count, 1)
    per_group = q_local // kv_local
    group = HEADS // KV_HEADS
    k_width = kv_local * HEAD_DIM
    scale = HEAD_DIM ** (-0.5)
    kv_first = tens_index * q_local // group * HEAD_DIM
    k_own = lax.dynamic_slice_in_dim(k_weight, kv_first, k_width, 1)
    v_own = lax.dynamic_slice_in_dim(v_weight, kv_first, k_width, 1)
    stream_f = stream_in.astype(f_wide)
    inv_rms = lax.rsqrt(jnp.mean(stream_f * stream_f, axis=-1, keepdims=True) + eps)
    unit_rows = stream_f * inv_rms
    normed = (unit_rows * gain).astype(f_low)
    rows_all = lax.all_gather(normed, "tensor", axis=0, tiled=True)
    weights = lax.all_gather(
        jnp.concatenate([q_weight, k_own, v_own], axis=1), "dp", axis=0, tiled=True
    )
    projected = jnp.dot(rows_all, weights, preferred_element_type=f_wide)
    block_first = data_index * tok_block
    seq_first = block_first // seq_len * seq_len
    places = block_first - seq_first + jnp.arange(tok_block, dtype=jnp.int32)
    query = rotate(
        projected[:, :q_width].reshape(tok_block, q_local, HEAD_DIM), places, 1.0
    ).astype(f_low)
    query = query.reshape(tok_block, kv_local, per_group, HEAD_DIM)
    keys_own = rotate(
        projected[:, q_width : q_width + k_width].reshape(tok_block, kv_local, HEAD_DIM),
        places,
        1.0,
    ).astype(f_low)
    values_own = projected[:, q_width + k_width :].astype(f_low)
    keys_all, values_all = (
        lax.all_gather(keys_own.reshape(tok_block, k_width), "dp", axis=0, tiled=True),
        lax.all_gather(values_own, "dp", axis=0, tiled=True),
    )
    keys = keys_all.reshape(seq_len, kv_local, HEAD_DIM)
    values = values_all.reshape(seq_len, kv_local, HEAD_DIM)
    key_place = jnp.arange(seq_len, dtype=jnp.int32)
    doc_query = lax.dynamic_slice_in_dim(doc_ids, block_first, tok_block)
    allowed = (key_place[None, :] <= places[:, None]) & (doc_ids[None, :] == doc_query[:, None])
    scores = jnp.einsum("qghd,kgd->ghqk", query, keys, preferred_element_type=f_wide) * scale
    scores = jnp.where(allowed[None, None], scores, -1e30)
    peak = jnp.max(scores, axis=-1, keepdims=True)
    exp_terms = jnp.exp(scores - peak)
    prob_rows = exp_terms / jnp.sum(exp_terms, axis=-1, keepdims=True)
    prob_low = prob_rows.astype(f_low)
    attended = jnp.einsum("ghqk,kgd->qghd", prob_low, values, preferred_element_type=f_wide).astype(
        f_low
    )
    attended = attended.reshape(tok_block, q_width)
    out_full = lax.all_gather(out_weight, "dp", axis=0, tiled=True)
    term = jnp.einsum("qc,dc->qd", attended, out_full, preferred_element_type=f_wide)
    rounded = lax.optimization_barrier(term.astype(f_low)).astype(f_wide)
    total = lax.psum_scatter(
        (pending[0].astype(f_wide) + rounded).astype(jnp.bfloat16),
        "tensor",
        scatter_dimension=0,
        tiled=True,
    ).astype(jnp.float32)
    hidden_out = (stream_f + total).astype(f_low)
    grad_all = lax.all_gather(grad_out, "tensor", axis=0, tiled=True)
    columns = grad_all
    grad_o = lax.psum_scatter(
        jnp.einsum("qd,qc->dc", columns, attended, preferred_element_type=f_wide).astype(
            jnp.bfloat16
        ),
        "dp",
        scatter_dimension=0,
        tiled=True,
    ).astype(jnp.float32)
    grad_heads = jnp.dot(grad_all, out_full, preferred_element_type=f_wide).astype(f_low)
    heads_split = grad_heads.reshape(tok_block, kv_local, per_group, HEAD_DIM)
    attn_split = attended.reshape(tok_block, kv_local, per_group, HEAD_DIM)
    delta = jnp.sum(heads_split.astype(f_wide) * attn_split.astype(f_wide), axis=-1)
    delta = jnp.transpose(delta, (1, 2, 0))[..., None]
    grad_prob = jnp.einsum("qghd,kgd->ghqk", heads_split, values, preferred_element_type=f_wide)
    grad_score = (prob_rows * (grad_prob - delta)).astype(f_low)
    grad_query = (
        jnp.einsum("ghqk,kgd->qghd", grad_score, keys, preferred_element_type=f_wide) * scale
    )
    grad_query = (
        rotate(grad_query.reshape(tok_block, q_local, HEAD_DIM), places, -1.0)
        .astype(f_low)
        .reshape(tok_block, q_width)
    )
    count = tok_block * lax.axis_size("dp")
    offset = jnp.int32(0) - seq_first
    score_part = window_keys(grad_score, offset, count, seq_len)
    prob_part = window_keys(prob_low, offset, count, seq_len)
    key_piece = (
        jnp.einsum("ghqk,qghd->kgd", score_part, query, preferred_element_type=f_wide) * scale
    )
    value_piece = jnp.einsum(
        "ghqk,qghd->kgd", prob_part, heads_split, preferred_element_type=f_wide
    )
    kv_grad = lax.psum_scatter(
        jnp.concatenate(
            [key_piece.reshape(count, k_width), value_piece.reshape(count, k_width)], axis=1
        ).astype(jnp.bfloat16),
        "dp",
        scatter_dimension=0,
        tiled=True,
    ).astype(jnp.float32)
    grad_key = rotate(
        kv_grad[:, :k_width].reshape(tok_block, kv_local, HEAD_DIM), places, -1.0
    ).astype(f_low)
    grad_key = grad_key.reshape(tok_block, k_width)
    grad_value = kv_grad[:, k_width:].astype(f_low)
    grad_proj = jnp.concatenate([grad_query, grad_key, grad_value], axis=1)
    columns = rows_all
    grad_w = lax.psum_scatter(
        jnp.einsum("qd,qc->dc", columns, grad_proj, preferred_element_type=f_wide).astype(
            jnp.bfloat16
        ),
        "dp",
        scatter_dimension=0,
        tiled=True,
    ).astype(jnp.float32)
    grad_q = grad_w[:, :q_width]
    blank = jnp.zeros((grad_w.shape[0], k_weight.shape[1]), f_wide)
    key_part = lax.dynamic_update_slice_in_dim(
        blank, grad_w[:, q_width : q_width + k_width], kv_first, 1
    )
    value_part = lax.dynamic_update_slice_in_dim(blank, grad_w[:, q_width + k_width :], kv_first, 1)
    grad_k, grad_v = (
        lax.psum(key_part.astype(jnp.bfloat16), "tensor").astype(jnp.float32),
        lax.psum(value_part.astype(jnp.bfloat16), "tensor").astype(jnp.float32),
    )
    normed_term = jnp.einsum("qc,dc->qd", grad_proj, weights, preferred_element_type=f_wide)
    grad_normed = lax.psum_scatter(
        normed_term.astype(jnp.bfloat16), "tensor", scatter_dimension=0, tiled=True
    ).astype(jnp.float32)
    grad_gain = lax.psum(jnp.sum(grad_normed * unit_rows, axis=0), ("dp", "tensor"))
    scaled_grad = grad_normed * gain
    grad_stream = (
        inv_rms
        * (scaled_grad - unit_rows * jnp.mean(scaled_grad * unit_rows, axis=-1, keepdims=True))
        + grad_out.astype(f_wide)
    ).astype(f_low)
    return (hidden_out, grad_stream, grad_gain, grad_q, grad_k, grad_v, grad_o)


def solution(mesh):
    in_specs = (
        P(("dp", "tensor"), None),
        P("tensor", "dp", None),
        P(),
        P("dp", "tensor"),
        P("dp", None),
        P("dp", None),
        P("dp", "tensor"),
        P(("dp", "tensor"), None),
        P(),
    )
    out_specs = (
        P(("dp", "tensor"), None),
        P(("dp", "tensor"), None),
        P(),
        P("dp", "tensor"),
        P("dp", None),
        P("dp", None),
        P("dp", "tensor"),
    )
    return jax.shard_map(
        on_device, mesh=mesh, in_specs=in_specs, out_specs=out_specs, check_vma=False
    )
```

profile of v0, /device:TPU:32, one launch (start us, length us, event | category | flops | bytes accessed | tf_op | source)
XLA Modules:
  0.0 1143.5 jit_solution(12878307090056131398)
XLA Ops:
  7.2 1.1 fusion.45
  8.3 1.7 fusion.42
  10.0 0.8 constant_dynamic-slice_fusion
  10.8 1.6 pad_maximum_fusion.1
  12.5 0.7 all-gather.17.cloned.1.call-update
  13.2 0.5 all-gather.15.cloned.1.call-update
  13.9 60.9 %all-gather.7.cloned.1.call-done = bf16[128,4096]{1,0:T(8,128)(2,1)} async-done(((bf16[16,4096]{1,0:T(8,128)(2,1)}), bf16[128,4096]{1,0:T(8,128)(2,1)}) %all-gather.7.cloned.1.call-update) | async-done | bytes 1048592 | tf_op jit(solution)/shard_map/all_gather | solution.py:59
  74.8 65.4 %all-gather.9.cloned.1.call-done = bf16[4096,768]{1,0:T(8,128)(2,1)} async-done(((bf16[128,768]{1,0:T(8,128)(2,1)}), bf16[4096,768]{1,0:T(8,128)(2,1)}) %all-gather.9.cloned.1.call-update) | async-done | bytes 6291472 | tf_op jit(solution)/shard_map/all_gather | solution.py:60
  140.2 4.1 fusion.80
  144.3 0.3 fusion.66
  144.6 0.7 pad_maximum_fusion.7
  145.5 0.3 broadcast_multiply_fusion
  145.8 1.9 fusion.20
  147.7 55.4 %all-gather.17.cloned.1.call-done = bf16[128,4096]{1,0:T(8,128)(2,1)} async-done(((bf16[16,4096]{1,0:T(8,128)(2,1)}), bf16[128,4096]{1,0:T(8,128)(2,1)}) %all-gather.17.cloned.1.call-update) | async-done | bytes 1048592 | tf_op jit(solution)/shard_map/all_gather | solution.py:106
  203.1 60.8 %all-gather.15.cloned.1.call-done = bf16[4096,512]{1,0:T(8,128)(2,1)} async-done(((bf16[128,512]{1,0:T(8,128)(2,1)}), bf16[4096,512]{1,0:T(8,128)(2,1)}) %all-gather.15.cloned.1.call-update) | async-done | bytes 4194320 | tf_op jit(solution)/shard_map/all_gather | solution.py:96
  263.9 3.2 convolution_convert_fusion.4
  267.2 0.1 copy.86
  267.3 0.1 copy.55
  267.4 0.6 slice.118
  268.1 0.2 fusion.78
  268.4 0.2 reduce-scatter.10.cloned.1.call-start
  268.7 55.4 %all-gather.13.cloned.1.call-done = bf16[4096,128]{1,0:T(8,128)(2,1)} async-done(((bf16[128,128]{1,0:T(8,128)(2,1)}), bf16[4096,128]{1,0:T(8,128)(2,1)}) %all-gather.13.cloned.1.call-update) | async-done | bytes 1048592 | tf_op jit(solution)/shard_map/all_gather | solution.py:78
  324.0 2.6 fusion.79
  326.6 1.1 fusion.3
  327.7 2.1 copy-done
  329.9 1.4 fusion.18
  331.3 2.0 copy-done.1
  333.3 2.3 fusion.9
  335.6 48.5 %all-gather.11.cloned.1.call-done = bf16[4096,128]{1,0:T(8,128)(2,1)} async-done(((bf16[128,128]{1,0:T(8,128)(2,1)}), bf16[4096,128]{1,0:T(8,128)(2,1)}) %all-gather.11.cloned.1.call-update) | async-done | bytes 1048592 | tf_op jit(solution)/shard_map/all_gather | solution.py:79
  384.1 3.4 multiply_reduce_fusion
  387.5 4.5 fusion.1
  392.1 2.3 fusion.8
  394.4 1.6 pad_maximum_fusion
  396.0 0.3 reduce-scatter.12.cloned.1.call-start
  396.3 3.9 fusion.24
  400.3 0.1 subtract_convert_fusion
  400.4 0.1 pad_maximum_fusion.4
  400.5 0.1 copy.59
  400.7 136.6 %reduce-scatter.10.cloned.1.call-done = bf16[128,256]{1,0:T(8,128)(2,1)} async-done(((bf16[4096,256]{1,0:T(8,128)(2,1)}), bf16[128,256]{1,0:T(8,128)(2,1)}) %reduce-scatter.10.cloned.1.call-update) | async-done | bytes 65552 | tf_op jit(solution)/shard_map/reduce_scatter | solution.py:141
  537.3 0.8 fusion.64
  538.1 0.3 fusion.68
  538.6 0.1 copy.68
  538.7 6.0 convolution_convert_fusion.2
  544.9 4.5 convolution_convert_fusion
  549.5 3.8 convolution_convert_fusion.3
  553.3 1.2 fusion.19
  554.6 3.3 fusion.4
  557.9 6.6 copy.82
  564.6 66.7 %reduce-scatter.12.cloned.1.call-done = bf16[16,4096]{1,0:T(8,128)(2,1)} async-done(((bf16[128,4096]{1,0:T(8,128)(2,1)}), bf16[16,4096]{1,0:T(8,128)(2,1)}) %reduce-scatter.12.cloned.1.call-update) | async-done | bytes 131088 | tf_op jit(solution)/shard_map/reduce_scatter | solution.py:175
  631.3 1.2 fusion.44
  632.4 150.7 %reduce-scatter.14.cloned.1.call-done = bf16[128,768]{1,0:T(8,128)(2,1)} async-done(((bf16[4096,768]{1,0:T(8,128)(2,1)}), bf16[128,768]{1,0:T(8,128)(2,1)}) %reduce-scatter.14.cloned.1.call-update) | async-done | bytes 196624 | tf_op jit(solution)/shard_map/reduce_scatter | solution.py:156
  783.1 0.8 slice_dynamic-update-slice_fusion
  783.9 0.8 slice_dynamic-update-slice_fusion.1
  784.8 0.6 copy-done.10
  785.4 88.9 %reduce-scatter.8.cloned.1.call-done = bf16[16,4096]{1,0:T(8,128)(2,1)} async-done(((bf16[128,4096]{1,0:T(8,128)(2,1)}), bf16[16,4096]{1,0:T(8,128)(2,1)}) %reduce-scatter.8.cloned.1.call-update) | async-done | bytes 131088 | tf_op jit(solution)/shard_map/reduce_scatter | solution.py:99
  874.3 1.8 fusion.41
  876.0 76.1 %psum.21 = f32[4096]{0:T(1024)} all-reduce(f32[4096]{0:T(1024)S(1)} %get-tuple-element.28), channel_id=1, replica_groups=mesh['dp'=32,'tensor'=8] {'dp','tensor'}, use_global_device_ids=true, to_apply=%region_9.10 | all-reduce | flops 4096 | bytes 32768 | tf_op jit(solution)/shard_map/psum | solution.py:178
  952.2 69.8 %reduce-scatter.16.cloned.1.call-done = bf16[128,512]{1,0:T(8,128)(2,1)} async-done(((bf16[4096,512]{1,0:T(8,128)(2,1)}), bf16[128,512]{1,0:T(8,128)(2,1)}) %reduce-scatter.16.cloned.1.call-update) | async-done | bytes 131088
  1021.9 1.0 copy.83
  1022.9 0.8 copy.69
  1023.8 1.6 slice.80
  1025.4 107.9 %all-reduce.5.cloned.1.call-done = (bf16[128,512]{1,0:T(8,128)(2,1)}, bf16[128,512]{1,0:T(8,128)(2,1)}) async-done(((bf16[128,512]{1,0:T(8,128)(2,1)}, bf16[128,512]{1,0:T(8,128)(2,1)}), (bf16[128,512]{1,0:T(8,128)(2,1)}, bf16[128,512]{1,0:T(8,128)(2,1)})) %all-reduce.5.cloned.1.call-update) | async-done | bytes 262160 | tf_op jit(solution)/shard_map/psum | solution.py:171
  1133.3 1.6 convert_element_type.175
  1135.0 1.6 convert_element_type.177
  (59 shorter events, 1.1 us)
Async XLA Ops:
  7.2 67.6 %all-gather.7.cloned.1.call-start = ((), (), s32[]{:S(2)}) async-start(), calls=%async_computation.5 | async-start | bytes 1179648 | tf_op jit(solution)/shard_map/all_gather | solution.py:59
  10.0 130.2 %all-gather.9.cloned.1.call-start = ((), (), s32[]{:S(2)}) async-start(), calls=%async_computation.6 | async-start | bytes 6488064 | tf_op jit(solution)/shard_map/all_gather | solution.py:60
  12.4 190.6 %all-gather.17.cloned.1.call-start = ((), (), s32[]{:S(2)}) async-start(), calls=%async_computation.11 | async-start | bytes 1179648 | tf_op jit(solution)/shard_map/all_gather | solution.py:106
  13.2 132.2 %copy-start.13 = (s32[4096]{0:T(1024)S(1)}, s32[4096]{0:T(1024)}, u32[]{:S(2)}) copy-start(s32[4096]{0:T(1024)} %param.17) | copy-start | bytes 49156
  13.2 250.7 %all-gather.15.cloned.1.call-start = ((), (), s32[]{:S(2)}) async-start(), calls=%async_computation.9 | async-start | bytes 4325376 | tf_op jit(solution)/shard_map/all_gather | solution.py:96
  13.8 310.3 %all-gather.13.cloned.1.call-start = ((), (), s32[]{:S(2)}) async-start(), calls=%async_computation.8 | async-start | bytes 1081344 | tf_op jit(solution)/shard_map/all_gather | solution.py:78
  145.3 238.8 %all-gather.11.cloned.1.call-start = ((), (), s32[]{:S(2)}) async-start(), calls=%async_computation.7 | async-start | bytes 1081344 | tf_op jit(solution)/shard_map/all_gather | solution.py:79
  268.4 268.9 %reduce-scatter.10.cloned.1.call-start = ((), (), s32[]{:S(2)}) async-start(), calls=%async_computation.12 | async-start | bytes 2162688 | tf_op jit(solution)/shard_map/reduce_scatter | solution.py:141
  326.6 3.3 copy-start
  331.3 2.0 copy-start.1
  384.1 3.4 copy-start.7
  392.1 2.4 copy-start.3
  394.4 1.9 copy-start.8
  396.0 235.2 %reduce-scatter.12.cloned.1.call-start = ((), (), s32[]{:S(2)}) async-start(), calls=%async_computation.13 | async-start | bytes 1179648 | tf_op jit(solution)/shard_map/reduce_scatter | solution.py:175
  538.7 6.1 copy-start.2
  544.8 238.3 %reduce-scatter.14.cloned.1.call-start = ((), (), s32[]{:S(2)}) async-start(), calls=%async_computation.14 | async-start | bytes 6488064 | tf_op jit(solution)/shard_map/reduce_scatter | solution.py:156
  549.4 3.9 copy-start.6
  549.4 324.9 %reduce-scatter.8.cloned.1.call-start = ((), (), s32[]{:S(2)}) async-start(), calls=%async_computation.10 | async-start | bytes 1179648 | tf_op jit(solution)/shard_map/reduce_scatter | solution.py:99
  549.5 5.1 copy-start.4
  554.6 467.4 %reduce-scatter.16.cloned.1.call-start = ((), (), s32[]{:S(2)}) async-start(), calls=%async_computation.15 | async-start | bytes 4325376
  564.5 66.8 %copy-start.5 = (bf16[16,4096]{1,0:T(8,128)(2,1)S(1)}, bf16[16,4096]{1,0:T(8,128)(2,1)}, u32[]{:S(2)}) copy-start(bf16[16,4096]{1,0:T(8,128)(2,1)} %param.9) | copy-start | bytes 393220
  564.5 66.8 %copy-start.12 = (f32[4096]{0:T(1024)S(1)}, f32[4096]{0:T(1024)}, u32[]{:S(2)}) copy-start(f32[4096]{0:T(1024)} %param.11) | copy-start | bytes 49156
  564.5 309.8 %copy-start.9 = (bf16[16,4096]{1,0:T(8,128)(2,1)S(1)}, bf16[16,4096]{1,0:T(8,128)(2,1)}, u32[]{:S(2)}) copy-start(bf16[16,4096]{1,0:T(8,128)(2,1)} %param.16) | copy-start | bytes 393220
  564.5 568.8 %all-reduce.5.cloned.1.call-start = ((), (), s32[]{:S(2)}) async-start(), calls=%async_computation.16 | async-start | bytes 524288 | tf_op jit(solution)/shard_map/psum | solution.py:171
  783.9 0.8 copy-start.11
  784.7 0.7 copy-start.10
Sparse Core Ops, SparseCore 0:
  11.2 63.5 all-gather.6
  77.2 62.8 all-gather.8
  142.8 60.2 all-gather.16
  204.8 59.0 all-gather.14
  266.2 57.7 all-gather.12
  326.3 57.7 all-gather.10
  396.2 141.0 reduce-scatter.9
  544.9 86.2 reduce-scatter.11
  633.8 149.2 reduce-scatter.13
  786.9 87.3 reduce-scatter.7
  877.0 144.8 reduce-scatter.15
  1025.2 108.0 all-reduce.4
where the time goes:
time: 1150 us; the launch traced here: 1140 us
  waiting for transfers between devices  968 us (84%)
  blocking collectives  76.1 us (7%)
  matrix products  44.1 us (4%)
  other arithmetic  20.5 us (2%)
  local copies, waits for them, and re-layouts  19 us (2%)
  between operations  14.6 us (1%)
    reduce_scatter x1, waiting for transfers between devices, on_device(): lax.psum_scatter(jnp.einsum('qd,qc->dc', columns, grad_proj, preferred_el...  151 us
    reduce_scatter x1, waiting for transfers between devices, on_device(): lax.psum_scatter(jnp.concatenate([key_piece.reshape(count, k_width), valu...  137 us
    psum x1, waiting for transfers between devices, on_device(): lax.psum(key_part.astype(jnp.bfloat16), 'tensor').astype(jnp.float32)  108 us
    reduce_scatter x1, waiting for transfers between devices, on_device(): lax.psum_scatter((pending[0].astype(f_wide) + rounded).astype(jnp.bfloat1...  88.9 us
    psum x1, blocking collectives, on_device(): lax.psum(jnp.sum(grad_normed * unit_rows, axis=0), ('dp', 'tensor'))  76.1 us
    unnamed x13, waiting for transfers between devices  71.1 us
    reduce_scatter x1, waiting for transfers between devices, on_device(): lax.psum_scatter(normed_term.astype(jnp.bfloat16), 'tensor', scatter_dime...  66.7 us
    all_gather x1, waiting for transfers between devices, on_device(): lax.all_gather(jnp.concatenate([q_weight, k_own, v_own], axis=1), 'dp', a...  65.4 us
  transfers between devices with their start and end apart: 12, of which 12 were waited for; matrix products, arithmetic and copies ran while one was open for 5% of the time, Pallas kernels for 0%

commit v1 on v0

v1 whole, which is shorter than its diff:
```python
import jax
import jax.numpy as jnp
from jax import lax
from jax.sharding import Mesh
from jax.sharding import PartitionSpec as P

HEADS = 32
KV_HEADS = 4
HEAD_DIM = 128
HALF_DIM = HEAD_DIM // 2

eps = 1e-05
rope_base = 500000.0

SIZES = {"y": 4, "z": 4, "c": 2, "h": 2, "x": 4}
DP = ("y", "z", "c")
TENSOR = ("h", "x")
wide = jnp.float32
low = jnp.bfloat16


def dot(a, b, dims):
    return lax.dot_general(a, b, (dims, ((), ())), preferred_element_type=wide)


def swap(a, axis):
    return lax.ppermute(a, axis, [(0, 1), (1, 0)])


def spread(a, axis):
    size = SIZES[axis]
    return lax.all_to_all(
        jnp.broadcast_to(a[None], (size,) + a.shape), axis, 0, 0, tiled=True
    )


def spread_yz(a):
    rows, cols = a.shape
    a = spread(a, "z").reshape(SIZES["z"] * rows, cols)
    return spread(a, "y").reshape(SIZES["y"] * SIZES["z"] * rows, cols)


def collect(a, axis):
    return jnp.sum(lax.all_to_all(a, axis, 0, 0, tiled=True).astype(wide), axis=0)


def collect_yz(a):
    rows, cols = a.shape
    a = collect(a.reshape(SIZES["y"], rows // SIZES["y"], cols), "y").astype(low)
    return collect(a.reshape(SIZES["z"], a.shape[0] // SIZES["z"], cols), "z")


def on_device(
    stream_in, pending, gain, q_weight, k_weight, v_weight, out_weight, grad_out, doc_ids
):
    y, z, c, h, x = (lax.axis_index(a) for a in ("y", "z", "c", "h", "x"))
    tens_index = h * SIZES["x"] + x
    rows_own, width = stream_in.shape
    tok = pending.shape[1]
    outer = SIZES["y"] * SIZES["z"]
    half_width = width // 2
    q_width = q_weight.shape[1]
    heads = q_width // HEAD_DIM
    seq_len = doc_ids.shape[0]
    scale = HEAD_DIM ** (-0.5)

    def columns(a, which):
        split = a.reshape(a.shape[0], outer, 2, width // outer // 2)
        return lax.dynamic_index_in_dim(split, which, 2, keepdims=False).reshape(
            a.shape[0], half_width
        )

    def spread_rows(a):
        pair = jnp.stack([columns(a, c), swap(columns(a, 1 - c), "c")])
        both = jnp.stack([pair, swap(pair, "h")])
        return spread(both, "x").reshape(2 * tok, half_width)

    def join(own, sibling):
        cols = own.shape[1]
        parts = [a.reshape(tok // rows_own, rows_own, cols) for a in (own, sibling)]
        return jnp.stack(parts, axis=1).reshape(2 * tok, cols)

    def join_cores(own):
        return join(own, swap(own, "c"))

    def sum_cores(a):
        split = a.reshape(tok // rows_own, 2, rows_own, a.shape[1])
        own, sibling = (split[:, i].reshape(tok, a.shape[1]) for i in range(2))
        return own + swap(sibling, "c")

    def collect_rows(a):
        a = collect(a.reshape(SIZES["x"], 2 * tok // SIZES["x"], half_width), "x")
        a = a.reshape(2, 2, rows_own, half_width)
        a = a[0] + swap(a[1].astype(low), "h").astype(wide)
        own, other = a[0], swap(a[1], "c")
        own, other = (b.reshape(rows_own, outer, 1, width // outer // 2) for b in (own, other))
        first, second = jnp.where(c == 0, own, other), jnp.where(c == 0, other, own)
        return jnp.concatenate([first, second], axis=2).reshape(rows_own, width)

    kv_first = tens_index * heads // (HEADS // KV_HEADS) * HEAD_DIM
    kv_weight = jnp.concatenate(
        [lax.dynamic_slice_in_dim(w, kv_first, HEAD_DIM, 1) for w in (k_weight, v_weight)], axis=1
    )
    wkv = spread_yz(kv_weight)
    wq = spread_yz(q_weight)
    wo = spread_yz(out_weight)

    stream_f = stream_in.astype(wide)
    inv_rms = lax.rsqrt(jnp.mean(stream_f * stream_f, axis=-1, keepdims=True) + eps)
    unit_rows = stream_f * inv_rms
    normed = spread_rows((unit_rows * gain).astype(low))
    grads = spread_rows(grad_out)

    rel_h = lax.broadcasted_iota(jnp.int32, (SIZES["x"], 2, rows_own), 1)
    at_x = lax.broadcasted_iota(jnp.int32, (SIZES["x"], 2, rows_own), 0)
    at_r = lax.broadcasted_iota(jnp.int32, (SIZES["x"], 2, rows_own), 2)
    local = (((h ^ rel_h) * SIZES["x"] + at_x) * rows_own + at_r).reshape(tok)
    block_first = ((y * SIZES["z"] + z) * 2 + c) * tok
    places = block_first + local
    rel_c = jnp.arange(2, dtype=jnp.int32)[:, None, None]
    at_yz = jnp.arange(outer, dtype=jnp.int32)[None, :, None]
    key_place = ((at_yz * 2 + (c ^ rel_c)) * tok + local[None, None, :]).reshape(seq_len)
    doc_block = lax.dynamic_slice_in_dim(doc_ids, block_first, tok)
    doc_block = doc_block.reshape(2, SIZES["x"], rows_own)
    doc_block = jnp.where(h == 0, doc_block, doc_block[::-1])
    doc_query = jnp.transpose(doc_block, (1, 0, 2)).reshape(tok)
    first_place = jnp.sum((doc_ids[None, :] < doc_query[:, None]).astype(jnp.int32), axis=1)
    allowed = (key_place[None, :] <= places[:, None]) & (key_place[None, :] >= first_place[:, None])

    frequency = rope_base ** (-2.0 * jnp.arange(HALF_DIM).astype(wide) / HEAD_DIM)
    angles = places.astype(wide)[:, None] * frequency[None, :]
    cosine, sine = jnp.cos(angles)[:, None, :], jnp.sin(angles)[:, None, :]

    def rotate(field, sign):
        first, second = field[..., :HALF_DIM], field[..., HALF_DIM:]
        return jnp.concatenate(
            [first * cosine - sign * second * sine, second * cosine + sign * first * sine], axis=-1
        )

    kv_proj = sum_cores(dot(normed, wkv, ((1,), (0,))))
    keys_own = rotate(kv_proj[:, :HEAD_DIM].reshape(tok, 1, HEAD_DIM), 1.0).reshape(tok, HEAD_DIM)
    kv_own = jnp.concatenate([keys_own, kv_proj[:, HEAD_DIM:]], axis=1).astype(low)
    kv_near = spread_yz(kv_own)
    kv_all = jnp.concatenate([kv_near, swap(kv_near, "c")], axis=0)
    keys, values = kv_all[:, :HEAD_DIM], kv_all[:, HEAD_DIM:]

    q_proj = sum_cores(dot(normed, wq, ((1,), (0,))))
    query = rotate(q_proj.reshape(tok, heads, HEAD_DIM), 1.0).astype(low)
    query = jnp.transpose(query, (1, 0, 2)).reshape(heads * tok, HEAD_DIM)
    grad_heads = sum_cores(dot(grads, wo, ((1,), (0,)))).astype(low)
    grad_heads = jnp.transpose(grad_heads.reshape(tok, heads, HEAD_DIM), (1, 0, 2))
    grad_heads = grad_heads.reshape(heads * tok, HEAD_DIM)

    scores = dot(query, keys, ((1,), (1,))).reshape(heads, tok, seq_len) * scale
    scores = jnp.where(allowed[None], scores, -1e30)
    peak = jnp.max(scores, axis=-1, keepdims=True)
    exp_terms = jnp.exp(scores - peak)
    prob = (exp_terms / jnp.sum(exp_terms, axis=-1, keepdims=True)).reshape(heads * tok, seq_len)
    prob_low = prob.astype(low)
    attended_h = dot(prob_low, values, ((1,), (0,))).astype(low)
    attended = jnp.transpose(attended_h.reshape(heads, tok, HEAD_DIM), (1, 0, 2))
    attended = join_cores(attended.reshape(tok, q_width))

    grad_o = collect_yz(dot(grads, attended, ((0,), (0,))).astype(low))

    delta = jnp.sum(grad_heads.astype(wide) * attended_h.astype(wide), axis=-1, keepdims=True)
    grad_prob = dot(grad_heads, values, ((1,), (1,)))
    grad_score = (prob * (grad_prob - delta)).astype(low)
    key_piece = dot(grad_score, query, ((0,), (0,))) * scale
    value_piece = dot(prob_low, grad_heads, ((0,), (0,)))
    kv_piece = jnp.concatenate([key_piece, value_piece], axis=1).astype(low)
    kv_sum = kv_piece[: seq_len // 2].astype(wide) + swap(kv_piece[seq_len // 2 :], "c").astype(wide)
    kv_grad = collect_yz(kv_sum.astype(low))

    grad_query = (dot(grad_score, keys, ((1,), (0,))) * scale).reshape(heads, tok, HEAD_DIM)
    grad_query = rotate(jnp.transpose(grad_query, (1, 0, 2)), -1.0).astype(low)
    grad_query = join_cores(grad_query.reshape(tok, q_width))
    grad_q = collect_yz(dot(normed, grad_query, ((0,), (0,))).astype(low))

    pend = pending[0].reshape(2, SIZES["x"], rows_own, width)
    pend = jnp.where(h == 0, pend, pend[::-1])
    pend = jnp.transpose(pend, (1, 0, 2, 3)).reshape(tok, width)
    pend = join(columns(pend, c), swap(columns(pend, 1 - c), "c"))
    terms = dot(attended, wo, ((1,), (1,))).astype(low).astype(wide)
    hidden_out = (stream_f + collect_rows((pend.astype(wide) + terms).astype(low))).astype(low)

    grad_key = rotate(kv_grad[:, :HEAD_DIM].reshape(tok, 1, HEAD_DIM), -1.0)
    grad_kv = jnp.concatenate([grad_key.reshape(tok, HEAD_DIM), kv_grad[:, HEAD_DIM:]], axis=1)
    grad_kv = join_cores(grad_kv.astype(low))
    grad_w_kv = collect_yz(dot(normed, grad_kv, ((0,), (0,))).astype(low))
    normed_terms = dot(grad_query, wq, ((1,), (1,))) + dot(grad_kv, wkv, ((1,), (1,)))
    grad_normed = collect_rows(normed_terms.astype(low))

    kv_blocks = spread(grad_w_kv.astype(low), "x").astype(wide)
    kv_blocks = (kv_blocks[0::2] + kv_blocks[1::2]).astype(low)
    kv_other = swap(kv_blocks, "h")
    kv_blocks = jnp.concatenate(
        [jnp.where(h == 0, kv_blocks, kv_other), jnp.where(h == 0, kv_other, kv_blocks)], axis=0
    ).astype(wide)
    grad_k, grad_v = (
        jnp.transpose(kv_blocks[:, :, i : i + HEAD_DIM], (1, 0, 2)).reshape(k_weight.shape)
        for i in (0, HEAD_DIM)
    )

    gain_part = jnp.sum(q_weight.astype(wide) * grad_q, axis=1)
    gain_part = gain_part + jnp.sum(kv_weight.astype(wide) * grad_w_kv, axis=1)
    gain_part = jnp.sum(spread(gain_part, "x"), axis=0)
    gain_part = gain_part + swap(gain_part, "h")
    gain_half = spread_yz(gain_part[None])
    gain_other = swap(gain_half, "c")
    grad_gain = jnp.stack(
        [jnp.where(c == 0, gain_half, gain_other), jnp.where(c == 0, gain_other, gain_half)], axis=1
    ).reshape(width) / gain

    scaled_grad = grad_normed * gain
    grad_stream = (
        inv_rms
        * (scaled_grad - unit_rows * jnp.mean(scaled_grad * unit_rows, axis=-1, keepdims=True))
        + grad_out.astype(wide)
    ).astype(low)
    return (hidden_out, grad_stream, grad_gain, grad_q, grad_k, grad_v, grad_o)


def solution(mesh):
    fine = Mesh(mesh.devices.reshape(tuple(SIZES.values())), tuple(SIZES))
    whole = P(DP + TENSOR, None)
    in_specs = (
        whole,
        P(TENSOR, DP, None),
        P(),
        P(DP, TENSOR),
        P(DP, None),
        P(DP, None),
        P(DP, TENSOR),
        whole,
        P(),
    )
    out_specs = (whole, whole, P(), P(DP, TENSOR), P(DP, None), P(DP, None), P(DP, TENSOR))
    return jax.shard_map(
        on_device, mesh=fine, in_specs=in_specs, out_specs=out_specs, check_vma=False
    )
```

time: 1150 us -> 509 us (0.44)
  waiting for transfers between devices: 968 us -> 187 us
  starting transfers between devices: 0.89 us -> 140 us
  blocking collectives: 76.1 us -> 19 us
  local copies, waits for them, and re-layouts: 19 us -> 65.2 us
  other arithmetic: 20.5 us -> 47.2 us
  between operations: 14.6 us -> 2.02 us
    reduce_scatter x4 -> x0, waiting for transfers between devices: 443 us -> none  [the longest x1 151 us: on_device(): lax.psum_scatter(jnp.einsum('qd,qc->dc', columns, grad_proj, preferred_el...]
    all_gather x6 -> x0, waiting for transfers between devices: 346 us -> none  [the longest x1 65.4 us: on_device(): lax.all_gather(jnp.concatenate([q_weight, k_own, v_own], axis=1), 'dp', a...]
    all_to_all x0 -> x23, waiting for transfers between devices: none -> 153 us  [the longest x13 81.3 us: spread(): lax.all_to_all(jnp.broadcast_to(a[None], (size,) + a.shape), axis, 0, 0,...]
    psum x1 -> x0, waiting for transfers between devices: 108 us -> none  [on_device(): lax.psum(key_part.astype(jnp.bfloat16), 'tensor').astype(jnp.float32)]
    all_to_all x0 -> x23, starting transfers between devices: none -> 104 us  [the longest x13 59.3 us: spread(): lax.all_to_all(jnp.broadcast_to(a[None], (size,) + a.shape), axis, 0, 0,...]
    psum x1 -> x0, blocking collectives: 76.1 us -> none  [on_device(): lax.psum(jnp.sum(grad_normed * unit_rows, axis=0), ('dp', 'tensor'))]
    unnamed x13 -> x0, waiting for transfers between devices: 71.1 us -> none
    ppermute x0 -> x20, starting transfers between devices: none -> 35.2 us  [swap(): return lax.ppermute(a, axis, [(0, 1), (1, 0)])]
  transfers between devices with their start and end apart: 12 -> 43, of which waited for: 12 -> 31; matrix products, arithmetic and copies ran while one was open for 5% -> 23% of each run, Pallas kernels for 0% -> 0%
where the time goes in v1:
time: 509 us; the launch traced here: 500 us
  waiting for transfers between devices  187 us (37%)
  starting transfers between devices  140 us (28%)
  local copies, waits for them, and re-layouts  65.2 us (13%)
  other arithmetic  47.2 us (9%)
  matrix products  40.1 us (8%)
  blocking collectives  19 us (4%)
    all_to_all x13, waiting for transfers between devices, spread(): lax.all_to_all(jnp.broadcast_to(a[None], (size,) + a.shape), axis, 0, 0,...  81.3 us
    all_to_all x10, waiting for transfers between devices, collect(): lax.all_to_all(a, axis, 0, 0, tiled=True).astype(wide)  71.6 us
    all_to_all x13, starting transfers between devices, spread(): lax.all_to_all(jnp.broadcast_to(a[None], (size,) + a.shape), axis, 0, 0,...  59.3 us
    all_to_all x10, starting transfers between devices, collect(): lax.all_to_all(a, axis, 0, 0, tiled=True).astype(wide)  45.1 us
    ppermute x20, starting transfers between devices, swap(): return lax.ppermute(a, axis, [(0, 1), (1, 0)])  35.2 us
    ppermute x20, waiting for transfers between devices, swap(): return lax.ppermute(a, axis, [(0, 1), (1, 0)])  34 us
    dot_general x14, matrix products, dot(): return lax.dot_general(a, b, (dims, ((), ())), preferred_element_type=wide)  31.7 us
    all_to_all x1, blocking collectives, spread(): lax.all_to_all(jnp.broadcast_to(a[None], (size,) + a.shape), axis, 0, 0,...  19 us
  transfers between devices with their start and end apart: 43, of which 31 were waited for; matrix products, arithmetic and copies ran while one was open for 23% of the time, Pallas kernels for 0%

profile of v1, /device:TPU:32, one launch (start us, length us, event | category | flops | bytes accessed | tf_op | source)
XLA Modules:
  0.0 500.1 jit_solution(2723272880948196932)
XLA Ops:
  2.3 6.0 %all-to-all-start.3 = ((bf16[4,128,256]{2,1,0:T(8,128)(2,1)}), bf16[4,128,256]{2,1,0:T(8,128)(2,1)S(1)}, u32[]{:S(2)}, u32[]{:S(2)}) async-start(bf16[4,128,256]{2,1,0:T(8,128)(2,1)} %broadcast_in_dim.51), calls=%async_computation.3 | async-start | bytes 524288 | tf_op jit(solution)/shard_map/all_to_all | solution.py:32
  9.4 6.0 %all-to-all-done.3 = bf16[4,128,256]{2,1,0:T(8,128)(2,1)S(1)} async-done(((bf16[4,128,256]{2,1,0:T(8,128)(2,1)}), bf16[4,128,256]{2,1,0:T(8,128)(2,1)S(1)}, u32[]{:S(2)}, u32[]{:S(2)}) %all-to-all-start.3) | async-done | bytes 262176 | tf_op jit(solution)/shard_map/all_to_all | solution.py:32
  17.1 5.9 %all-to-all-start.1 = ((bf16[4,128,512]{2,1,0:T(8,128)(2,1)}), bf16[4,128,512]{2,1,0:T(8,128)(2,1)}, u32[]{:S(2)}, u32[]{:S(2)}) async-start(bf16[4,128,512]{2,1,0:T(8,128)(2,1)} %broadcast_in_dim.48), calls=%async_computation.1 | async-start | bytes 1048576 | tf_op jit(solution)/shard_map/all_to_all | solution.py:32
  26.4 5.0 %collective-permute-start.2 = (bf16[2,16,2048]{2,1,0:T(8,128)(2,1)S(1)}, bf16[2,16,2048]{2,1,0:T(8,128)(2,1)S(1)}, u32[]{:S(2)}, u32[]{:S(2)}) collective-permute-start(bf16[2,16,2048]{2,1,0:T(8,128)(2,1)S(1)} %get-tuple-element.81), channel_id=1, source_target_pairs={{0,4},{4,0},{1,5},{5,1},{2,6},{6,2},{3,7},{7,3},{8,12},{12,8},{9,1... | collective-permute-start | bytes 393224 | tf_op jit(solution)/shard_map/ppermute | solution.py:27
  31.4 7.3 %collective-permute-done.2 = bf16[2,16,2048]{2,1,0:T(8,128)(2,1)S(1)} collective-permute-done((bf16[2,16,2048]{2,1,0:T(8,128)(2,1)S(1)}, bf16[2,16,2048]{2,1,0:T(8,128)(2,1)S(1)}, u32[]{:S(2)}, u32[]{:S(2)}) %collective-permute-start.2) | collective-permute-done | bytes 131104 | tf_op jit(solution)/shard_map/ppermute | solution.py:27
  38.9 19.0 %all_to_all.121 = bf16[4,2,2,16,2048]{4,3,2,1,0:T(8,128)(2,1)S(1)} all-to-all(bf16[4,2,2,16,2048]{4,3,2,1,0:T(8,128)(2,1)S(1)} %broadcast_in_dim.47), channel_id=1, replica_groups=mesh['y'=4,'z'=4,'c'=2,'h'=2,'x'=4] {'x'}, dimensions={0} | all-to-all | bytes 2097152 | tf_op jit(solution)/shard_map/all_to_all | solution.py:32
  59.0 4.5 all-to-all-start.4
  64.4 12.8 %all-to-all-done.4 = bf16[4,512,256]{2,1,0:T(8,128)(2,1)S(1)} async-done(((bf16[4,512,256]{2,1,0:T(8,128)(2,1)}), bf16[4,512,256]{2,1,0:T(8,128)(2,1)S(1)}, u32[]{:S(2)}, u32[]{:S(2)}) %all-to-all-start.4) | async-done | bytes 1048608 | tf_op jit(solution)/shard_map/all_to_all | solution.py:32
  78.0 6.6 %all-to-all-start.7 = ((bf16[4,128,512]{2,1,0:T(8,128)(2,1)}), bf16[4,128,512]{2,1,0:T(8,128)(2,1)S(1)}, u32[]{:S(2)}, u32[]{:S(2)}) async-start(bf16[4,128,512]{2,1,0:T(8,128)(2,1)} %broadcast_in_dim.62), calls=%async_computation.7 | async-start | bytes 1048576 | tf_op jit(solution)/shard_map/all_to_all | solution.py:32
  84.6 4.2 collective-permute-start.10
  90.1 8.1 %collective-permute-done.10 = bf16[2,16,2048]{2,1,0:T(8,128)(2,1)} collective-permute-done((bf16[2,16,2048]{2,1,0:T(8,128)(2,1)S(1)}, bf16[2,16,2048]{2,1,0:T(8,128)(2,1)}, u32[]{:S(2)}, u32[]{:S(2)}) %collective-permute-start.10) | collective-permute-done | bytes 131104 | tf_op jit(solution)/shard_map/ppermute | solution.py:27
  100.7 3.5 all-to-all-start.10
  106.9 11.1 %all-to-all-done.10 = bf16[4,2,2,16,2048]{4,3,2,1,0:T(8,128)(2,1)S(1)} async-done(((bf16[4,2,2,16,2048]{4,3,2,1,0:T(8,128)(2,1)}), bf16[4,2,2,16,2048]{4,3,2,1,0:T(8,128)(2,1)S(1)}, u32[]{:S(2)}, u32[]{:S(2)}) %all-to-all-start.10) | async-done | bytes 1048608 | tf_op jit(solution)/shard_map/all_to_all | solution.py:32
  118.7 5.7 %all-to-all-start.5 = ((bf16[4,128,256]{2,1,0:T(8,128)(2,1)}), bf16[4,128,256]{2,1,0:T(8,128)(2,1)S(1)}, u32[]{:S(2)}, u32[]{:S(2)}) async-start(bf16[4,128,256]{2,1,0:T(8,128)(2,1)} %broadcast_in_dim.58), calls=%async_computation.5 | async-start | bytes 524288 | tf_op jit(solution)/shard_map/all_to_all | solution.py:32
  126.7 3.9 all-to-all-done.5
  133.2 4.7 all-to-all-start.2
  142.5 5.1 %dynamic-slice_reduce_fusion = (bf16[128,16,128]{2,1,0:T(8,128)(2,1)}, bf16[128,16,1,128]{3,2,1,0:T(2,128)(2,1)}) fusion(bf16[128,16,2,128]{3,2,1,0:T(2,128)(2,1)S(1)} %reshape_reshape.4, s32[]{:T(128)S(6)} %select_n.123, s32[]{:T(128)S(6)} %select_n.124), kind=kLoop, calls=%fused_computation.50 | loop fusion | bytes 2097160 | tf_op jit(solution)/shard_map/jit(dynamic_index_in_dim)/dynamic_slice | solution.py:69
  147.6 3.5 copy.239
  152.1 6.4 %all-to-all-done.2 = bf16[4,512,512]{2,1,0:T(8,128)(2,1)} async-done(((bf16[4,512,512]{2,1,0:T(8,128)(2,1)}), bf16[4,512,512]{2,1,0:T(8,128)(2,1)}, u32[]{:S(2)}, u32[]{:S(2)}) %all-to-all-start.2) | async-done | bytes 2097184 | tf_op jit(solution)/shard_map/all_to_all | solution.py:32
  161.1 4.6 all-to-all-start.8
  167.4 3.1 fusion.75
  170.5 16.4 %all-to-all-done.8 = bf16[4,512,512]{2,1,0:T(8,128)(2,1)} async-done(((bf16[4,512,512]{2,1,0:T(8,128)(2,1)}), bf16[4,512,512]{2,1,0:T(8,128)(2,1)}, u32[]{:S(2)}, u32[]{:S(2)}) %all-to-all-start.8) | async-done | bytes 2097184 | tf_op jit(solution)/shard_map/all_to_all | solution.py:32
  187.9 3.5 all-to-all-start.6
  198.1 4.3 all-to-all-done.6
  220.1 8.4 %fusion.69 = (f32[4,128]{1,0:T(4,128)}, f32[4,128,4096]{2,1,0:T(8,128)}) fusion(pred[128,4096]{1,0:T(8,128)(4,1)} %compare_and_fusion, bf16[4096,128]{1,0:T(8,128)(2,1)} %fusion.17, bf16[128,4,128]{2,0,1:T(8,128)(2,1)S(1)} %pad_maximum_fusion.11), kind=kOutput, calls=%fused_computation.171 | convolution fusion | flops 545263616 | bytes 10094592 | tf_op jit(solution)/shard_map/sub | solution.py:157
  228.5 4.4 broadcast_divide_fusion
  234.4 3.3 multiply_reduce_fusion.1
  251.0 4.1 fusion.12
  255.0 4.3 all-to-all-start.9
  259.3 3.8 convolution_multiply_fusion.1
  265.9 9.5 %all-to-all-done.9 = bf16[4,64,2048]{2,1,0:T(8,128)(2,1)} async-done(((bf16[4,64,2048]{2,1,0:T(8,128)(2,1)}), bf16[4,64,2048]{2,1,0:T(8,128)(2,1)}, u32[]{:S(2)}, u32[]{:S(2)}) %all-to-all-start.9) | async-done | bytes 1048608 | tf_op jit(solution)/shard_map/all_to_all | solution.py:44
  275.4 3.5 all-to-all-start.11
  285.7 8.4 %all-to-all-done.11 = bf16[4,512,256]{1,2,0:T(8,128)(2,1)S(1)} async-done(((bf16[4,512,256]{1,2,0:T(8,128)(2,1)}), bf16[4,512,256]{1,2,0:T(8,128)(2,1)S(1)}, u32[]{:S(2)}, u32[]{:S(2)}) %all-to-all-start.11) | async-done | bytes 1048608 | tf_op jit(solution)/shard_map/all_to_all | solution.py:44
  295.2 4.4 all-to-all-start.14
  303.6 21.7 %all-to-all-done.14 = bf16[4,512,512]{2,1,0:T(8,128)(2,1)} async-done(((bf16[4,512,512]{2,1,0:T(8,128)(2,1)}), bf16[4,512,512]{2,1,0:T(8,128)(2,1)}, u32[]{:S(2)}, u32[]{:S(2)}) %all-to-all-start.14) | async-done | bytes 2097184 | tf_op jit(solution)/shard_map/all_to_all | solution.py:44
  325.2 4.6 all-to-all-start.12
  332.9 3.3 all-to-all-done.12
  336.2 4.5 all-to-all-start.22
  342.8 8.0 %collective-permute-start.7 = (bf16[2,16,2048]{2,1,0:T(8,128)(2,1)}, bf16[2,16,2048]{2,1,0:T(8,128)(2,1)}, u32[]{:S(2)}, u32[]{:S(2)}) collective-permute-start(bf16[2,16,2048]{2,1,0:T(8,128)(2,1)} %bitcast.41), channel_id=1, source_target_pairs={{0,4},{4,0},{1,5},{5,1},{2,6},{6,2},{3,7},{7,3},{8,12},{12,8},{9,1... | collective-permute-start | bytes 393224 | tf_op jit(solution)/shard_map/ppermute | solution.py:27
  356.0 8.2 %all-to-all-done.22 = bf16[4,512,512]{2,1,0:T(8,128)(2,1)} async-done(((bf16[4,512,512]{2,1,0:T(8,128)(2,1)}), bf16[4,512,512]{2,1,0:T(8,128)(2,1)}, u32[]{:S(2)}, u32[]{:S(2)}) %all-to-all-start.22) | async-done | bytes 2097184 | tf_op jit(solution)/shard_map/all_to_all | solution.py:44
  364.2 4.0 all-to-all-start.15
  373.2 3.5 all-to-all-done.15
  376.7 3.5 all-to-all-start.16
  382.3 3.3 fusion.9
  385.6 6.7 %all-to-all-done.16 = bf16[4,512,256]{2,1,0:T(8,128)(2,1)S(1)} async-done(((bf16[4,512,256]{2,1,0:T(8,128)(2,1)}), bf16[4,512,256]{2,1,0:T(8,128)(2,1)S(1)}, u32[]{:S(2)}, u32[]{:S(2)}) %all-to-all-start.16) | async-done | bytes 1048608 | tf_op jit(solution)/shard_map/all_to_all | solution.py:44
  392.4 3.5 all-to-all-start.13
  401.1 5.7 %all-to-all-done.13 = bf16[4,64,2048]{2,1,0:T(8,128)(2,1)S(1)} async-done(((bf16[4,64,2048]{2,1,0:T(8,128)(2,1)}), bf16[4,64,2048]{2,1,0:T(8,128)(2,1)S(1)}, u32[]{:S(2)}, u32[]{:S(2)}) %all-to-all-start.13) | async-done | bytes 1048608 | tf_op jit(solution)/shard_map/all_to_all | solution.py:44
  406.8 5.4 %all-to-all-start.23 = ((bf16[4,128,512]{2,1,0:T(8,128)(2,1)}), bf16[4,128,512]{2,1,0:T(8,128)(2,1)S(1)}, u32[]{:S(2)}, u32[]{:S(2)}) async-start(bf16[4,128,512]{2,1,0:T(8,128)(2,1)} %bitcast.216), calls=%async_computation.23 | async-start | bytes 1048576 | tf_op jit(solution)/shard_map/all_to_all | solution.py:44
  414.5 8.1 %collective-permute-start.15 = (bf16[2,16,2048]{2,1,0:T(8,128)(2,1)S(1)}, bf16[2,16,2048]{2,1,0:T(8,128)(2,1)S(1)}, u32[]{:S(2)}, u32[]{:S(2)}) collective-permute-start(bf16[2,16,2048]{2,1,0:T(8,128)(2,1)S(1)} %bitcast.250), channel_id=1, source_target_pairs={{0,4},{4,0},{1,5},{5,1},{2,6},{6,2},{3,7},{7,3},{8,12},{12,8},{9,1... | collective-permute-start | bytes 393224 | tf_op jit(solution)/shard_map/ppermute | solution.py:27
  423.7 4.4 collective-permute-done.15
  428.1 7.4 %all-to-all-start.17 = ((bf16[4,128,256]{2,1,0:T(8,128)(2,1)}), bf16[4,128,256]{2,1,0:T(8,128)(2,1)S(1)}, u32[]{:S(2)}, u32[]{:S(2)}) async-start(bf16[4,128,256]{2,1,0:T(8,128)(2,1)} %bitcast.77), calls=%async_computation.17 | async-start | bytes 524288 | tf_op jit(solution)/shard_map/all_to_all | solution.py:44
  437.1 4.6 all-to-all-done.17
  442.5 3.7 all-to-all-start.18
  446.2 5.2 %all-to-all-done.18 = f32[4,1,128]{2,1,0:T(1,128)S(1)} async-done(((f32[4,1,128]{2,1,0:T(1,128)}), f32[4,1,128]{2,1,0:T(1,128)S(1)}, u32[]{:S(2)}, u32[]{:S(2)}) %all-to-all-start.18) | async-done | bytes 2080 | tf_op jit(solution)/shard_map/all_to_all | solution.py:32
  451.4 3.9 collective-permute-start.17
  455.7 3.2 collective-permute-done.17
  459.5 4.0 all-to-all-start.19
  463.7 3.8 all-to-all-done.19
  468.1 3.2 all-to-all-start.20
  471.4 5.3 %all-to-all-done.20 = f32[4,4,128]{2,1,0:T(4,128)S(1)} async-done(((f32[4,4,128]{2,1,0:T(4,128)}), f32[4,4,128]{2,1,0:T(4,128)S(1)}, u32[]{:S(2)}, u32[]{:S(2)}) %all-to-all-start.20) | async-done | bytes 8224 | tf_op jit(solution)/shard_map/all_to_all | solution.py:32
  477.4 3.4 all-to-all-start.21
  481.6 5.8 %all-to-all-done.21 = bf16[4,128,256]{2,1,0:T(8,128)(2,1)S(1)} async-done(((bf16[4,128,256]{2,1,0:T(8,128)(2,1)}), bf16[4,128,256]{2,1,0:T(8,128)(2,1)S(1)}, u32[]{:S(2)}, u32[]{:S(2)}) %all-to-all-start.21) | async-done | bytes 262176 | tf_op jit(solution)/shard_map/all_to_all | solution.py:32
  487.7 3.9 collective-permute-start.19
  492.2 5.8 %collective-permute-done.19 = bf16[2,128,256]{1,2,0:T(8,128)(2,1)S(1)} collective-permute-done((bf16[2,128,256]{1,2,0:T(8,128)(2,1)S(1)}, bf16[2,128,256]{1,2,0:T(8,128)(2,1)S(1)}, u32[]{:S(2)}, u32[]{:S(2)}) %collective-permute-start.19) | collective-permute-done | bytes 131104 | tf_op jit(solution)/shard_map/ppermute | solution.py:27
  (271 shorter events, 121.2 us)
Async XLA Ops:
  0.6 22.4 %copy-start.8 = (bf16[16,4096]{1,0:T(8,128)(2,1)S(1)}, bf16[16,4096]{1,0:T(8,128)(2,1)}, u32[]{:S(2)}) copy-start(bf16[16,4096]{1,0:T(8,128)(2,1)} %param.9) | copy-start | bytes 393220
  0.6 22.4 %copy-start.26 = (f32[4096]{0:T(1024)S(1)}, f32[4096]{0:T(1024)}, u32[]{:S(2)}) copy-start(f32[4096]{0:T(1024)} %param.11) | copy-start | bytes 49156
  0.7 22.6 %copy-start.18 = (bf16[16,4096]{1,0:T(8,128)(2,1)S(1)}, bf16[16,4096]{1,0:T(8,128)(2,1)}, u32[]{:S(2)}) copy-start(bf16[16,4096]{1,0:T(8,128)(2,1)} %param.16) | copy-start | bytes 393220
  1.6 23.4 %copy-start.22 = (bf16[128,128]{1,0:T(8,128)(2,1)}, bf16[128,128]{1,0:T(8,128)(2,1)S(1)}, u32[]{:S(2)}) copy-start(bf16[128,128]{1,0:T(8,128)(2,1)S(1)} %get-tuple-element.97) | copy-start | bytes 98308
  1.6 23.4 %copy-start.24 = (bf16[128,128]{1,0:T(8,128)(2,1)}, bf16[128,128]{1,0:T(8,128)(2,1)S(1)}, u32[]{:S(2)}) copy-start(bf16[128,128]{1,0:T(8,128)(2,1)S(1)} %get-tuple-element.98) | copy-start | bytes 98308
  2.3 13.1 %all-to-all-start.3 = ((bf16[4,128,256]{2,1,0:T(8,128)(2,1)}), bf16[4,128,256]{2,1,0:T(8,128)(2,1)S(1)}, u32[]{:S(2)}, u32[]{:S(2)}) async-start(bf16[4,128,256]{2,1,0:T(8,128)(2,1)} %broadcast_in_dim.51), calls=%async_computation.3 | async-start | bytes 524288 | tf_op jit(solution)/shard_map/all_to_all | solution.py:32
  9.4 13.8 %copy-start.31 = (f32[16]{0:T(128)}, f32[16]{0:T(128)S(1)}, u32[]{:S(2)}) copy-start(f32[16]{0:T(128)S(1)} %add_rsqrt_fusion) | copy-start | bytes 196
  17.1 21.7 %all-to-all-start.1 = ((bf16[4,128,512]{2,1,0:T(8,128)(2,1)}), bf16[4,128,512]{2,1,0:T(8,128)(2,1)}, u32[]{:S(2)}, u32[]{:S(2)}) async-start(bf16[4,128,512]{2,1,0:T(8,128)(2,1)} %broadcast_in_dim.48), calls=%async_computation.1 | async-start | bytes 1048576 | tf_op jit(solution)/shard_map/all_to_all | solution.py:32
  25.0 1.3 collective-permute-start.1
  26.4 12.4 %collective-permute-start.2 = (bf16[2,16,2048]{2,1,0:T(8,128)(2,1)S(1)}, bf16[2,16,2048]{2,1,0:T(8,128)(2,1)S(1)}, u32[]{:S(2)}, u32[]{:S(2)}) collective-permute-start(bf16[2,16,2048]{2,1,0:T(8,128)(2,1)S(1)} %get-tuple-element.81), channel_id=1, source_target_pairs={{0,4},{4,0},{1,5},{5,1},{2,6},{6,2},{3,7},{7,3},{8,12},{12,8},{9,1... | collective-permute-start | bytes 393224 | tf_op jit(solution)/shard_map/ppermute | solution.py:27
  57.9 19.3 %copy-start.28 = (bf16[128,512]{1,0:T(8,128)(2,1)S(1)}, bf16[128,512]{1,0:T(8,128)(2,1)}, u32[]{:S(2)}) copy-start(bf16[128,512]{1,0:T(8,128)(2,1)} %param.15) | copy-start | bytes 393220
  59.0 18.2 %all-to-all-start.4 = ((bf16[4,512,256]{2,1,0:T(8,128)(2,1)}), bf16[4,512,256]{2,1,0:T(8,128)(2,1)S(1)}, u32[]{:S(2)}, u32[]{:S(2)}) async-start(bf16[4,512,256]{2,1,0:T(8,128)(2,1)} %broadcast_in_dim.57), calls=%async_computation.4 | async-start | bytes 2097152 | tf_op jit(solution)/shard_map/all_to_all | solution.py:32
  63.5 21.1 %collective-permute-start.9 = (bf16[16,2048]{1,0:T(8,128)(2,1)S(1)}, bf16[16,2048]{1,0:T(8,128)(2,1)S(1)}, u32[]{:S(2)}, u32[]{:S(2)}) collective-permute-start(bf16[16,2048]{1,0:T(8,128)(2,1)S(1)} %bitcast.256), channel_id=1, source_target_pairs={{0,8},{8,0},{1,9},{9,1},{2,10},{10,2},{3,11},{11,3},{4,12},{12,4},... | collective-permute-start | bytes 196616 | tf_op jit(solution)/shard_map/ppermute | solution.py:27
  63.8 20.8 %copy-start.34 = (s32[128]{0:T(128)}, s32[128]{0:T(128)S(1)}, u32[]{:S(2)}) copy-start(s32[128]{0:T(128)S(1)} %add.186) | copy-start | bytes 1540
  78.0 21.5 %all-to-all-start.7 = ((bf16[4,128,512]{2,1,0:T(8,128)(2,1)}), bf16[4,128,512]{2,1,0:T(8,128)(2,1)S(1)}, u32[]{:S(2)}, u32[]{:S(2)}) async-start(bf16[4,128,512]{2,1,0:T(8,128)(2,1)} %broadcast_in_dim.62), calls=%async_computation.7 | async-start | bytes 1048576 | tf_op jit(solution)/shard_map/all_to_all | solution.py:32
  84.6 13.5 %collective-permute-start.10 = (bf16[2,16,2048]{2,1,0:T(8,128)(2,1)S(1)}, bf16[2,16,2048]{2,1,0:T(8,128)(2,1)}, u32[]{:S(2)}, u32[]{:S(2)}) collective-permute-start(bf16[2,16,2048]{2,1,0:T(8,128)(2,1)S(1)} %get-tuple-element.79), channel_id=1, source_target_pairs={{0,4},{4,0},{1,5},{5,1},{2,6},{6,2},{3,7},{7,3},{8,12},{12,8},{9,1... | collective-permute-start | bytes 393224 | tf_op jit(solution)/shard_map/ppermute | solution.py:27
  90.1 14.8 %collective-permute-start.4 = (f32[128,256]{0,1:T(8,128)}, f32[128,256]{0,1:T(8,128)}, u32[]{:S(2)}, u32[]{:S(2)}) collective-permute-start(f32[128,256]{0,1:T(8,128)} %copy.249), channel_id=1, source_target_pairs={{0,8},{8,0},{1,9},{9,1},{2,10},{10,2},{3,11},{11,3},{4,12},{12,4},... | collective-permute-start | bytes 393224 | tf_op jit(solution)/shard_map/ppermute | solution.py:27
  100.7 17.3 %all-to-all-start.10 = ((bf16[4,2,2,16,2048]{4,3,2,1,0:T(8,128)(2,1)}), bf16[4,2,2,16,2048]{4,3,2,1,0:T(8,128)(2,1)S(1)}, u32[]{:S(2)}, u32[]{:S(2)}) async-start(bf16[4,2,2,16,2048]{4,3,2,1,0:T(8,128)(2,1)} %broadcast_in_dim.65), calls=%async_computation.10 | async-start | bytes 2097152 | tf_op jit(solution)/shard_map/all_to_all | solution.py:32
  117.9 15.2 %copy-start.3 = (bf16[4,2,2,16,2048]{4,3,2,1,0:T(8,128)(2,1)}, bf16[4,2,2,16,2048]{4,3,2,1,0:T(8,128)(2,1)S(1)}, u32[]{:S(2)}) copy-start(bf16[4,2,2,16,2048]{4,3,2,1,0:T(8,128)(2,1)S(1)} %all-to-all-done.10) | copy-start | bytes 3145732
  118.7 11.9 %all-to-all-start.5 = ((bf16[4,128,256]{2,1,0:T(8,128)(2,1)}), bf16[4,128,256]{2,1,0:T(8,128)(2,1)S(1)}, u32[]{:S(2)}, u32[]{:S(2)}) async-start(bf16[4,128,256]{2,1,0:T(8,128)(2,1)} %broadcast_in_dim.58), calls=%async_computation.5 | async-start | bytes 524288 | tf_op jit(solution)/shard_map/all_to_all | solution.py:32
  133.2 25.4 %all-to-all-start.2 = ((bf16[4,512,512]{2,1,0:T(8,128)(2,1)}), bf16[4,512,512]{2,1,0:T(8,128)(2,1)}, u32[]{:S(2)}, u32[]{:S(2)}) async-start(bf16[4,512,512]{2,1,0:T(8,128)(2,1)} %broadcast_in_dim.50), calls=%async_computation.2 | async-start | bytes 4194304 | tf_op jit(solution)/shard_map/all_to_all | solution.py:32
  151.0 54.8 %collective-permute-start = (bf16[128,2048]{0,1:T(8,128)(2,1)}, bf16[128,2048]{0,1:T(8,128)(2,1)}, u32[]{:S(2)}, u32[]{:S(2)}) collective-permute-start(bf16[128,2048]{0,1:T(8,128)(2,1)} %bitcast.2), channel_id=1, source_target_pairs={{0,8},{8,0},{1,9},{9,1},{2,10},{10,2},{3,11},{11,3},{4,12},{12,4},... | collective-permute-start | bytes 1572872 | tf_op jit(solution)/shard_map/ppermute | solution.py:27
  161.1 25.8 %all-to-all-start.8 = ((bf16[4,512,512]{2,1,0:T(8,128)(2,1)}), bf16[4,512,512]{2,1,0:T(8,128)(2,1)}, u32[]{:S(2)}, u32[]{:S(2)}) async-start(bf16[4,512,512]{2,1,0:T(8,128)(2,1)} %broadcast_in_dim.64), calls=%async_computation.8 | async-start | bytes 4194304 | tf_op jit(solution)/shard_map/all_to_all | solution.py:32
  187.9 14.4 %all-to-all-start.6 = ((bf16[4,512,256]{2,1,0:T(8,128)(2,1)}), bf16[4,512,256]{2,1,0:T(8,128)(2,1)S(1)}, u32[]{:S(2)}, u32[]{:S(2)}) async-start(bf16[4,512,256]{2,1,0:T(8,128)(2,1)} %broadcast_in_dim.60), calls=%async_computation.6 | async-start | bytes 2097152 | tf_op jit(solution)/shard_map/all_to_all | solution.py:32
  194.1 14.8 %collective-permute-start.3 = (f32[128,512]{0,1:T(8,128)}, f32[128,512]{0,1:T(8,128)}, u32[]{:S(2)}, u32[]{:S(2)}) collective-permute-start(f32[128,512]{0,1:T(8,128)} %copy.245), channel_id=1, source_target_pairs={{0,8},{8,0},{1,9},{9,1},{2,10},{10,2},{3,11},{11,3},{4,12},{12,4},... | collective-permute-start | bytes 786440 | tf_op jit(solution)/shard_map/ppermute | solution.py:27
  194.1 8.6 %copy-start.33 = (f32[64]{0:T(128)S(1)}, f32[64]{0:T(128)}, u32[]{:S(2)}) copy-start(f32[64]{0:T(128)} %multiply_power_fusion) | copy-start | bytes 772
  197.6 15.6 %collective-permute-start.11 = (f32[128,512]{1,0:T(8,128)}, f32[128,512]{1,0:T(8,128)}, u32[]{:S(2)}, u32[]{:S(2)}) collective-permute-start(f32[128,512]{1,0:T(8,128)} %bitcast.50), channel_id=1, source_target_pairs={{0,8},{8,0},{1,9},{9,1},{2,10},{10,2},{3,11},{11,3},{4,12},{12,4},... | collective-permute-start | bytes 786440 | tf_op jit(solution)/shard_map/ppermute | solution.py:27
  202.3 15.6 %collective-permute-start.5 = (bf16[2048,256]{1,0:T(8,128)(2,1)S(1)}, bf16[2048,256]{1,0:T(8,128)(2,1)}, u32[]{:S(2)}, u32[]{:S(2)}) collective-permute-start(bf16[2048,256]{1,0:T(8,128)(2,1)S(1)} %bitcast.197), channel_id=1, source_target_pairs={{0,8},{8,0},{1,9},{9,1},{2,10},{10,2},{3,11},{11,3},{4,12},{12,4},... | collective-permute-start | bytes 3145736 | tf_op jit(solution)/shard_map/ppermute | solution.py:27
  217.9 10.6 %copy-start.15 = (bf16[128,4,128]{2,0,1:T(8,128)(2,1)}, bf16[128,4,128]{2,0,1:T(8,128)(2,1)S(1)}, u32[]{:S(2)}) copy-start(bf16[128,4,128]{2,0,1:T(8,128)(2,1)S(1)} %pad_maximum_fusion.11) | copy-start | bytes 393220
  243.2 20.0 %collective-permute-start.13 = (bf16[2048,256]{0,1:T(8,128)(2,1)}, bf16[2048,256]{0,1:T(8,128)(2,1)}, u32[]{:S(2)}, u32[]{:S(2)}) collective-permute-start(bf16[2048,256]{0,1:T(8,128)(2,1)} %pad_maximum_fusion), channel_id=1, source_target_pairs={{0,8},{8,0},{1,9},{9,1},{2,10},{10,2},{3,11},{11,3},{4,12},{12,4},... | collective-permute-start | bytes 3145736 | tf_op jit(solution)/shard_map/ppermute | solution.py:27
  244.4 3.8 collective-permute-start.6
  255.0 20.3 %all-to-all-start.9 = ((bf16[4,64,2048]{2,1,0:T(8,128)(2,1)}), bf16[4,64,2048]{2,1,0:T(8,128)(2,1)}, u32[]{:S(2)}, u32[]{:S(2)}) async-start(bf16[4,64,2048]{2,1,0:T(8,128)(2,1)} %bitcast.207), calls=%async_computation.9 | async-start | bytes 2097152 | tf_op jit(solution)/shard_map/all_to_all | solution.py:44
  275.4 18.7 %all-to-all-start.11 = ((bf16[4,512,256]{1,2,0:T(8,128)(2,1)}), bf16[4,512,256]{1,2,0:T(8,128)(2,1)S(1)}, u32[]{:S(2)}, u32[]{:S(2)}) async-start(bf16[4,512,256]{1,2,0:T(8,128)(2,1)} %bitcast.206), calls=%async_computation.11 | async-start | bytes 2097152 | tf_op jit(solution)/shard_map/all_to_all | solution.py:44
  280.8 1.7 collective-permute-start.12
  295.2 30.1 %all-to-all-start.14 = ((bf16[4,512,512]{2,1,0:T(8,128)(2,1)}), bf16[4,512,512]{2,1,0:T(8,128)(2,1)}, u32[]{:S(2)}, u32[]{:S(2)}) async-start(bf16[4,512,512]{2,1,0:T(8,128)(2,1)} %bitcast.74), calls=%async_computation.14 | async-start | bytes 4194304 | tf_op jit(solution)/shard_map/all_to_all | solution.py:44
  299.6 30.2 %copy-start.4 = (bf16[4,2,2,16,2048]{4,3,2,1,0:T(8,128)(2,1)S(1)}, bf16[4,2,2,16,2048]{4,3,2,1,0:T(8,128)(2,1)}, u32[]{:S(2)}) copy-start(bf16[4,2,2,16,2048]{4,3,2,1,0:T(8,128)(2,1)} %copy-done.3) | copy-start | bytes 3145732
  325.2 10.9 %all-to-all-start.12 = ((bf16[4,128,256]{1,2,0:T(8,128)(2,1)}), bf16[4,128,256]{1,2,0:T(8,128)(2,1)}, u32[]{:S(2)}, u32[]{:S(2)}) async-start(bf16[4,128,256]{1,2,0:T(8,128)(2,1)} %copy_bitcast_fusion.1), calls=%async_computation.12 | async-start | bytes 524288 | tf_op jit(solution)/shard_map/all_to_all | solution.py:44
  336.2 28.0 %all-to-all-start.22 = ((bf16[4,512,512]{2,1,0:T(8,128)(2,1)}), bf16[4,512,512]{2,1,0:T(8,128)(2,1)}, u32[]{:S(2)}, u32[]{:S(2)}) async-start(bf16[4,512,512]{2,1,0:T(8,128)(2,1)} %bitcast.90), calls=%async_computation.22 | async-start | bytes 4194304 | tf_op jit(solution)/shard_map/all_to_all | solution.py:44
  342.1 22.1 %copy-start.9 = (f32[64,2048]{1,0:T(8,128)}, f32[64,2048]{1,0:T(8,128)S(1)}, u32[]{:S(2)}) copy-start(f32[64,2048]{1,0:T(8,128)S(1)} %convert_reduce_fusion.1) | copy-start | bytes 1572868
  342.8 37.4 %collective-permute-start.7 = (bf16[2,16,2048]{2,1,0:T(8,128)(2,1)}, bf16[2,16,2048]{2,1,0:T(8,128)(2,1)}, u32[]{:S(2)}, u32[]{:S(2)}) collective-permute-start(bf16[2,16,2048]{2,1,0:T(8,128)(2,1)} %bitcast.41), channel_id=1, source_target_pairs={{0,4},{4,0},{1,5},{5,1},{2,6},{6,2},{3,7},{7,3},{8,12},{12,8},{9,1... | collective-permute-start | bytes 393224 | tf_op jit(solution)/shard_map/ppermute | solution.py:27
  364.2 12.5 %all-to-all-start.15 = ((bf16[4,128,512]{2,1,0:T(8,128)(2,1)}), bf16[4,128,512]{2,1,0:T(8,128)(2,1)S(1)}, u32[]{:S(2)}, u32[]{:S(2)}) async-start(bf16[4,128,512]{2,1,0:T(8,128)(2,1)} %bitcast.75), calls=%async_computation.15 | async-start | bytes 1048576 | tf_op jit(solution)/shard_map/all_to_all | solution.py:44
  370.2 1.3 collective-permute-start.14
  376.7 15.7 %all-to-all-start.16 = ((bf16[4,512,256]{2,1,0:T(8,128)(2,1)}), bf16[4,512,256]{2,1,0:T(8,128)(2,1)S(1)}, u32[]{:S(2)}, u32[]{:S(2)}) async-start(bf16[4,512,256]{2,1,0:T(8,128)(2,1)} %bitcast.76), calls=%async_computation.16 | async-start | bytes 2097152 | tf_op jit(solution)/shard_map/all_to_all | solution.py:44
  385.6 10.3 %copy-start.12 = (f32[2,16,2048]{2,1,0:T(8,128)S(1)}, f32[2,16,2048]{2,1,0:T(8,128)}, u32[]{:S(2)}) copy-start(f32[2,16,2048]{2,1,0:T(8,128)} %convert_add_fusion.2) | copy-start | bytes 786436
  392.4 14.4 %all-to-all-start.13 = ((bf16[4,64,2048]{2,1,0:T(8,128)(2,1)}), bf16[4,64,2048]{2,1,0:T(8,128)(2,1)S(1)}, u32[]{:S(2)}, u32[]{:S(2)}) async-start(bf16[4,64,2048]{2,1,0:T(8,128)(2,1)} %bitcast.69), calls=%async_computation.13 | async-start | bytes 2097152 | tf_op jit(solution)/shard_map/all_to_all | solution.py:44
  395.9 1.4 collective-permute-start.8
  406.8 21.3 %all-to-all-start.23 = ((bf16[4,128,512]{2,1,0:T(8,128)(2,1)}), bf16[4,128,512]{2,1,0:T(8,128)(2,1)S(1)}, u32[]{:S(2)}, u32[]{:S(2)}) async-start(bf16[4,128,512]{2,1,0:T(8,128)(2,1)} %bitcast.216), calls=%async_computation.23 | async-start | bytes 1048576 | tf_op jit(solution)/shard_map/all_to_all | solution.py:44
  414.5 13.5 %collective-permute-start.15 = (bf16[2,16,2048]{2,1,0:T(8,128)(2,1)S(1)}, bf16[2,16,2048]{2,1,0:T(8,128)(2,1)S(1)}, u32[]{:S(2)}, u32[]{:S(2)}) collective-permute-start(bf16[2,16,2048]{2,1,0:T(8,128)(2,1)S(1)} %bitcast.250), channel_id=1, source_target_pairs={{0,4},{4,0},{1,5},{5,1},{2,6},{6,2},{3,7},{7,3},{8,12},{12,8},{9,1... | collective-permute-start | bytes 393224 | tf_op jit(solution)/shard_map/ppermute | solution.py:27
  422.7 13.7 %copy-start.10 = (f32[128,512]{1,0:T(8,128)}, f32[128,512]{1,0:T(8,128)S(1)}, u32[]{:S(2)}) copy-start(f32[128,512]{1,0:T(8,128)S(1)} %convert_reduce_fusion.4) | copy-start | bytes 786436
  422.7 13.7 %copy-start.17 = (bf16[128,512]{1,0:T(8,128)(2,1)S(1)}, bf16[128,512]{1,0:T(8,128)(2,1)}, u32[]{:S(2)}) copy-start(bf16[128,512]{1,0:T(8,128)(2,1)} %param.12) | copy-start | bytes 393220
  423.6 18.1 %copy-start.23 = (bf16[128,128]{1,0:T(8,128)(2,1)S(1)}, bf16[128,128]{1,0:T(8,128)(2,1)}, u32[]{:S(2)}) copy-start(bf16[128,128]{1,0:T(8,128)(2,1)} %copy-done.22) | copy-start | bytes 98308
  423.6 18.1 %copy-start.25 = (bf16[128,128]{1,0:T(8,128)(2,1)S(1)}, bf16[128,128]{1,0:T(8,128)(2,1)}, u32[]{:S(2)}) copy-start(bf16[128,128]{1,0:T(8,128)(2,1)} %copy-done.24) | copy-start | bytes 98308
  428.1 13.7 %all-to-all-start.17 = ((bf16[4,128,256]{2,1,0:T(8,128)(2,1)}), bf16[4,128,256]{2,1,0:T(8,128)(2,1)S(1)}, u32[]{:S(2)}, u32[]{:S(2)}) async-start(bf16[4,128,256]{2,1,0:T(8,128)(2,1)} %bitcast.77), calls=%async_computation.17 | async-start | bytes 524288 | tf_op jit(solution)/shard_map/all_to_all | solution.py:44
  435.5 27.9 %copy-start.32 = (f32[16]{0:T(128)S(1)}, f32[16]{0:T(128)}, u32[]{:S(2)}) copy-start(f32[16]{0:T(128)} %copy-done.31) | copy-start | bytes 196
  435.5 1.4 collective-permute-start.16
  436.5 44.2 %copy-start.11 = (f32[16,4096]{1,0:T(8,128)S(1)}, f32[16,4096]{1,0:T(8,128)}, u32[]{:S(2)}) copy-start(f32[16,4096]{1,0:T(8,128)} %reshape.658) | copy-start | bytes 786436
  436.5 44.2 %copy-start.19 = (bf16[16,4096]{1,0:T(8,128)(2,1)S(1)}, bf16[16,4096]{1,0:T(8,128)(2,1)}, u32[]{:S(2)}) copy-start(bf16[16,4096]{1,0:T(8,128)(2,1)} %param.16) | copy-start | bytes 393220
  442.5 8.9 %all-to-all-start.18 = ((f32[4,1,128]{2,1,0:T(1,128)}), f32[4,1,128]{2,1,0:T(1,128)S(1)}, u32[]{:S(2)}, u32[]{:S(2)}) async-start(f32[4,1,128]{2,1,0:T(1,128)} %broadcast_in_dim.66), calls=%async_computation.18 | async-start | bytes 4096 | tf_op jit(solution)/shard_map/all_to_all | solution.py:32
  451.4 7.5 %collective-permute-start.17 = (f32[128]{0:T(128)S(1)}, f32[128]{0:T(128)S(1)}, u32[]{:S(2)}, u32[]{:S(2)}) collective-permute-start(f32[128]{0:T(128)S(1)} %reduce_sum.189), channel_id=1, source_target_pairs={{0,4},{4,0},{1,5},{5,1},{2,6},{6,2},{3,7},{7,3},{8,12},{12,8},{9,1... | collective-permute-start | bytes 1544 | tf_op jit(solution)/shard_map/ppermute | solution.py:27
  459.5 8.0 %all-to-all-start.19 = ((f32[4,1,128]{2,1,0:T(1,128)}), f32[4,1,128]{2,1,0:T(1,128)S(1)}, u32[]{:S(2)}, u32[]{:S(2)}) async-start(f32[4,1,128]{2,1,0:T(1,128)} %broadcast_in_dim.67), calls=%async_computation.19 | async-start | bytes 4096 | tf_op jit(solution)/shard_map/all_to_all | solution.py:32
  468.1 8.5 %all-to-all-start.20 = ((f32[4,4,128]{2,1,0:T(4,128)}), f32[4,4,128]{2,1,0:T(4,128)S(1)}, u32[]{:S(2)}, u32[]{:S(2)}) async-start(f32[4,4,128]{2,1,0:T(4,128)} %broadcast_in_dim.69), calls=%async_computation.20 | async-start | bytes 16384 | tf_op jit(solution)/shard_map/all_to_all | solution.py:32
  477.4 10.1 %all-to-all-start.21 = ((bf16[4,128,256]{2,1,0:T(8,128)(2,1)}), bf16[4,128,256]{2,1,0:T(8,128)(2,1)S(1)}, u32[]{:S(2)}, u32[]{:S(2)}) async-start(bf16[4,128,256]{2,1,0:T(8,128)(2,1)} %broadcast_in_dim.70), calls=%async_computation.21 | async-start | bytes 524288 | tf_op jit(solution)/shard_map/all_to_all | solution.py:32
  481.6 10.0 %collective-permute-start.18 = (f32[16,128]{1,0:T(8,128)S(1)}, f32[16,128]{1,0:T(8,128)S(1)}, u32[]{:S(2)}, u32[]{:S(2)}) collective-permute-start(f32[16,128]{1,0:T(8,128)S(1)} %bitcast.260), channel_id=1, source_target_pairs={{0,8},{8,0},{1,9},{9,1},{2,10},{10,2},{3,11},{11,3},{4,12},{12,4},... | collective-permute-start | bytes 24584 | tf_op jit(solution)/shard_map/ppermute | solution.py:27
  487.7 10.4 %collective-permute-start.19 = (bf16[2,128,256]{1,2,0:T(8,128)(2,1)S(1)}, bf16[2,128,256]{1,2,0:T(8,128)(2,1)S(1)}, u32[]{:S(2)}, u32[]{:S(2)}) collective-permute-start(bf16[2,128,256]{1,2,0:T(8,128)(2,1)S(1)} %add_convert_fusion.1), channel_id=1, source_target_pairs={{0,4},{4,0},{1,5},{5,1},{2,6},{6,2},{3,7},{7,3},{8,12},{12,8},{9,1... | collective-permute-start | bytes 393224 | tf_op jit(solution)/shard_map/ppermute | solution.py:27
  (17 other events, 69.5 us)
